TPU v7x, 256 devices: a whole 4x4x8 slice. The times are simulated.
256 devices in a mesh: row: 64 (over y, z_hi, x), col: 4 (over z_lo, core).
Axes of the slice: x: 4, y: 4, z: 8 (z_hi: 4, z_lo: 2; z = z_hi * 2 + z_lo), core: 2. Of those that a mesh axis runs over, the one named last changes fastest.
Arguments:
- cotangent: bfloat16 [1024, 28672], P('col', 'row'), may hold values from -0.1875 to 0.1875
- activations: bfloat16 [1024, 8192], P('col', 'row'), may hold values from -6 to 6
- shard_of_token: int32 [1024], P('col'), may hold values from 0 to 2047
- shard_weight: float32 [2048], replicated, may hold values from 0.25 to 4
- hidden_basis: bfloat16 [28672, 28672], P('row', 'col'), may hold values from -0.03125 to 0.03125
- input_basis: bfloat16 [8192, 8192], P('col', 'row'), may hold values from -0.0625 to 0.0625
- eigenvalues: bfloat16 [28672, 8192], P('col', 'row'), may hold values from 0.099609375 to 2
- panel_order: int32 [2], replicated, may hold values from 0 to 111, as said below
Outputs:
- influence_direction: bfloat16 [28672, 8192], P('row', 'col')
Inputs may be any that keep to these rules, and one draw needn't show every extreme that they name: `panel_order`: the 2 panels of the window are all different, and the last panel, number 28672 / 256 - 1, is always one of them.
All inputs are finite; a program needn't handle non-finite values.
Results may differ from a plain program's by a relative error of at most 0.025.
Values may be sent and summed in bfloat16 or wider, within the bound.
A program may use at most 128 MiB of HBM per device.

v0:
```python
import jax
import jax.numpy as jnp
from jax import lax
from jax.sharding import PartitionSpec as P

PANEL = 256
STEPS = 2


DAMPING = 0.01


def spread(block, axis, owner):
    block = jnp.where(lax.axis_index(axis) == owner, block, jnp.zeros_like(block))
    return lax.psum(block, axis)


def rotate_columns(basis_window, grad_cols):
    return lax.dot_general(
        basis_window.astype(jnp.float32),
        grad_cols,
        (((0,), (1,)), ((), ())),
        precision=lax.Precision.HIGHEST,
    )


def per_device(
    cotangent,
    activations,
    shard_of_token,
    shard_weight,
    hidden_basis,
    input_basis,
    eigenvalues,
    panel_order,
):
    shard_ids = lax.broadcasted_iota(jnp.int32, (1, shard_weight.shape[0]), 1)
    matches = shard_of_token[:, None] == shard_ids
    token_weight = jnp.sum(jnp.where(matches, shard_weight[None, :], 0.0), axis=1)
    scaled = (cotangent.astype(jnp.float32) * token_weight[:, None]).astype(jnp.bfloat16)
    full_rows = lax.all_gather(activations, "row", axis=1, tiled=True)
    per_col = hidden_basis.shape[1] // PANEL
    basis_parts = []
    eigen_parts = []
    for step in range(STEPS):
        chosen = panel_order[step]
        owner = chosen // per_col
        offset = chosen % per_col * PANEL
        basis_piece = lax.dynamic_slice_in_dim(hidden_basis, offset, PANEL, 1)
        eigen_piece = lax.dynamic_slice_in_dim(eigenvalues, offset, PANEL, 0)
        basis_piece, eigen_piece = (
            spread(basis_piece, "col", owner),
            spread(eigen_piece, "col", owner),
        )
        basis_parts.append(basis_piece)
        eigen_parts.append(eigen_piece)
    basis_window = jnp.concatenate(basis_parts, axis=1)
    eigen_window = jnp.concatenate(eigen_parts, axis=0)
    grad_cols = lax.psum_scatter(
        lax.dot_general(
            full_rows, scaled, (((0,), (0,)), ((), ())), preferred_element_type=jnp.float32
        ).astype(jnp.bfloat16),
        "col",
        scatter_dimension=0,
        tiled=True,
    ).astype(jnp.float32)
    rotated = lax.psum(rotate_columns(basis_window, grad_cols), "row").astype(jnp.bfloat16)
    turn_term = jnp.dot(rotated, input_basis, preferred_element_type=jnp.float32)
    turned = lax.psum(turn_term.astype(jnp.bfloat16), "col").astype(jnp.float32)
    coefficients = (turned / (eigen_window.astype(jnp.float32) + DAMPING)).astype(jnp.bfloat16)
    return_term = lax.dot_general(
        coefficients, input_basis, (((1,), (1,)), ((), ())), preferred_element_type=jnp.float32
    )
    returned = lax.psum(return_term, "row").astype(jnp.bfloat16)
    return jnp.dot(basis_window, returned, preferred_element_type=jnp.float32).astype(jnp.bfloat16)


def solution(mesh):
    placed = (
        P("col", "row"),
        P("col", "row"),
        P("col"),
        P(),
        P("row", "col"),
        P("col", "row"),
        P("col", "row"),
        P(),
    )
    return jax.shard_map(
        per_device, mesh=mesh, in_specs=placed, out_specs=P("row", "col"), check_vma=False
    )
```

profile of v0, /device:TPU:6, one launch (start us, length us, event | category | flops | bytes accessed | tf_op | source)
XLA Modules:
  0.0 1125.8 jit_solution(2733703929051307968)
XLA Ops:
  7.4 0.0 copy-start
  7.4 0.0 all-gather.2.cloned.1.call-start
  7.4 0.7 all-gather.2.cloned.1.call-update
  8.1 0.0 all-reduce.9.cloned.1.call-start
  8.1 1.3 fusion.15
  13.4 1.9 dynamic-slice_select_fusion
  15.3 0.0 all-reduce.9.cloned.1.call-update
  15.3 0.0 reduce-scatter.2.cloned.1.call-start
  15.3 1.1 select_reduce_fusion
  16.4 103.9 %all-gather.2.cloned.1.call-done = bf16[256,8192]{1,0:T(8,128)(2,1)} async-done(((bf16[256,128]{1,0:T(8,128)(2,1)}), bf16[256,8192]{1,0:T(8,128)(2,1)}) %all-gather.2.cloned.1.call-update) | async-done | bytes 4194320 | tf_op jit(solution)/shard_map/all_gather | solution.py:41
  120.3 7.4 fusion
  127.7 0.0 reduce-scatter.2.cloned.1.call-update
  127.7 0.0 all-reduce.7.cloned.1.call-start
  127.7 1.6 dynamic-slice_select_fusion.3
  129.3 0.0 all-reduce.9.cloned.1.call-done
  129.3 1.0 constant_dynamic-update-slice_fusion.1
  130.3 1.0 constant_dynamic-update-slice_fusion
  131.2 68.2 %reduce-scatter.2.cloned.1.call-done = bf16[2048,448]{0,1:T(8,128)(2,1)} async-done(((bf16[8192,448]{0,1:T(8,128)(2,1)}), bf16[2048,448]{0,1:T(8,128)(2,1)}) %reduce-scatter.2.cloned.1.call-update) | async-done | bytes 1835024 | tf_op jit(solution)/shard_map/reduce_scatter | solution.py:59
  199.4 4.7 fusion.16
  204.1 425.7 %all-reduce.10 = bf16[512,2048]{1,0:T(8,128)(2,1)S(1)} all-reduce(f32[512,2048]{1,0:T(8,128)} %fusion.16), channel_id=1, replica_groups=mesh['row'=64,'col'=4] {'row'}, use_global_device_ids=true, to_apply=%region_4.5 | all-reduce | flops 1048576 | bytes 6291456 | tf_op jit(solution)/shard_map/psum | solution.py:67
  629.8 0.0 copy-done
  629.9 1.4 fusion.4
  631.2 0.0 all-reduce.7.cloned.1.call-update
  631.2 53.5 %all-reduce.7.cloned.1.call-done = (bf16[512,128]{1,0:T(8,128)(2,1)}, bf16[256,128]{1,0:T(8,128)(2,1)}, bf16[256,128]{1,0:T(8,128)(2,1)}) async-done(((bf16[512,128]{1,0:T(8,128)(2,1)}, bf16[256,128]{1,0:T(8,128)(2,1)}, bf16[256,128]{1,0:T(8,128)(2,1)}), (bf16[512,128]{1,0:T(8,128)(2,1)}, bf16[256,128]{1,0:T(8,128)(2,1)}, bf16[256,128]{1,0:T(8,128)(2,1)})) %all-reduce.7.cloned.1.call-update) | async-done | bytes 262160 | tf_op jit(solution)/shard_map/psum | solution.py:69
  684.8 3.6 fusion.8
  688.3 427.5 %all-reduce.11 = bf16[512,2048]{1,0:T(8,128)(2,1)S(1)} all-reduce(f32[512,2048]{1,0:T(8,128)} %fusion.8), channel_id=1, replica_groups=mesh['row'=64,'col'=4] {'row'}, use_global_device_ids=true, to_apply=%region_8.9 | all-reduce | flops 1048576 | bytes 6291456 | tf_op jit(solution)/shard_map/psum | solution.py:74
  1115.9 2.4 convolution_convert_fusion.1
Async XLA Ops:
  7.4 622.5 %copy-start = (bf16[2048,128]{1,0:T(8,128)(2,1)S(1)}, bf16[2048,128]{1,0:T(8,128)(2,1)}, u32[]{:S(2)}) copy-start(bf16[2048,128]{1,0:T(8,128)(2,1)} %param.13) | copy-start | bytes 1572868
  7.4 112.9 %all-gather.2.cloned.1.call-start = ((), (), s32[]{:S(2)}) async-start(), calls=%async_computation.1 | async-start | bytes 4259840 | tf_op jit(solution)/shard_map/all_gather | solution.py:41
  8.1 121.2 %all-reduce.9.cloned.1.call-start = ((), (), s32[]{:S(2)}) async-start(), calls=%async_computation.4 | async-start | bytes 917504 | tf_op jit(solution)/shard_map/psum | solution.py:15
  15.3 184.1 %reduce-scatter.2.cloned.1.call-start = ((), (), s32[]{:S(2)}) async-start(), calls=%async_computation.2 | async-start | bytes 9175040 | tf_op jit(solution)/shard_map/reduce_scatter | solution.py:59
  127.7 557.1 %all-reduce.7.cloned.1.call-start = ((), (), s32[]{:S(2)}) async-start(), calls=%async_computation.3 | async-start | bytes 524288 | tf_op jit(solution)/shard_map/psum | solution.py:69
Sparse Core Ops, SparseCore 0:
  11.8 108.4 all-gather.1
Sparse Core Ops, SparseCore 1:
  15.4 46.2 all-reduce.8
  127.8 71.6 reduce-scatter.1
  631.3 53.4 all-reduce.6
where the time goes:
time: 1140 us; the launch traced here: 1130 us
  blocking collectives  853 us (75%)
  waiting for transfers between devices  226 us (20%)
  matrix products  19.4 us (2%)
  between operations  19 us (2%)
    psum x1, blocking collectives, per_device(): returned = lax.psum(return_term, 'row').astype(jnp.bfloat16)  428 us
    psum x1, blocking collectives, per_device(): lax.psum(rotate_columns(basis_window, grad_cols), 'row')  426 us
    all_gather x1, waiting for transfers between devices, per_device(): full_rows = lax.all_gather(activations, 'row', axis=1, tiled=True)  104 us
    reduce_scatter x1, waiting for transfers between devices, per_device(): lax.psum_scatter(lax.dot_general(full_rows, scaled, (((0,), (0,)), ((), (...  68.2 us
    psum x1, waiting for transfers between devices, per_device(): turned = lax.psum(turn_term.astype(jnp.bfloat16), 'col').astype(jnp.float32)  53.5 us
  transfers between devices with their start and end apart: 4, of which 3 were waited for; matrix products, arithmetic and copies ran while one was open for 1% of the time, Pallas kernels for 0%

commit v1 on v0

v1 whole, which is shorter than its diff:
```python
import jax
import jax.numpy as jnp
from jax import lax
from jax.experimental import pallas as pl
from jax.experimental.pallas import tpu as pltpu
from jax.sharding import PartitionSpec as P

PANEL = 256
LAST = 111
PER_COL = 28
DAMPING = 0.01
MESH = pl.DeviceIdType.MESH
F32 = jnp.float32
BF16 = jnp.bfloat16

(S_ACT, S_BAS, S_EIX, S_EIC, S_H, S_PX, S_PY, S_PZ, S_PG, S_RC, S_RZ, S_RY, S_TC, S_CC, S_QY, S_QZ,
 S_GZ, S_GY0, S_GX0, S_GX1, S_GY1, N_STAGES) = range(22)


def pick(order_hbm, hid_hbm, eig_hbm, h_src, e_src, order, sems):
    col = lax.axis_index("col")
    cp = pltpu.make_async_copy(order_hbm, order, sems.at[0])
    cp.start()
    cp.wait()
    other = order[0] + order[1] - LAST
    place = pl.multiple_of((other - col * PER_COL) * PANEL, PANEL)
    mine = (other >= col * PER_COL) & (other < (col + 1) * PER_COL)
    end = (PER_COL - 1) * PANEL

    def fetch(have, at, k):
        h_part = h_src.at[:, PANEL * k:PANEL * (k + 1)]
        e_part = e_src.at[PANEL * k:PANEL * (k + 1)]

        def copies():
            return (pltpu.make_async_copy(hid_hbm.at[:, pl.ds(at, PANEL)], h_part, sems.at[1 + 2 * k]),
                    pltpu.make_async_copy(eig_hbm.at[pl.ds(at, PANEL)], e_part, sems.at[2 + 2 * k]))

        @pl.when(have)
        def _():
            for cp in copies():
                cp.start()

        @pl.when(jnp.logical_not(have))
        def _():
            h_part[...] = jnp.zeros(h_part.shape, BF16)
            e_part[...] = jnp.zeros(e_part.shape, BF16)

        @pl.when(have)
        def _():
            for cp in copies():
                cp.wait()

    fetch(mine, place, 0)
    fetch(col == 3, end, 1)


def kernel(
    cot_hbm, act_hbm, shard_hbm, weight_hbm, bas_hbm, h_src, e_src, out_hbm,
    cot_t, cot, shard_ref, weight_ref, act_g, bas_g,
    e_x, e_c,
    h_a, h_b, h_win,
    p_src, p_x, p_y0, p_y, p_z0, p_z, p_g,
    r_src, r_c, r_full,
    t_src, t_c, c_all,
    q_src, q_y, q_z0, q_z, ret,
    out_buf,
    ssem, rsem, lsem, osem,
):
    row = lax.axis_index("row")
    col = lax.axis_index("col")
    x = row % 4
    zh = (row // 4) % 4
    y = row // 16
    core = col % 2

    def at_x(j):
        return (y * 16 + zh * 4 + j, col)

    def at_y(j):
        return (j * 16 + zh * 4 + x, col)

    def at_z(j):
        return (y * 16 + j * 4 + x, col)

    def at_c(j):
        return (row, j)

    sends = []

    def send(stage, slot, src, dst, sem_at, device):
        cp = pltpu.make_async_remote_copy(
            src_ref=src, dst_ref=dst, send_sem=ssem.at[stage, slot], recv_sem=rsem.at[stage, sem_at],
            device_id=device, device_id_type=MESH)
        cp.start()
        sends.append(cp)

    def arrived(stage, sem_at, dst, device):
        pltpu.make_async_remote_copy(
            src_ref=dst, dst_ref=dst, send_sem=ssem.at[stage, 0], recv_sem=rsem.at[stage, sem_at],
            device_id=device, device_id_type=MESH).wait_recv()

    def start(stage, me, place, src_of, dst):
        for d in (2, 1, 3):
            j = (me + d) % 4
            send(stage, d, src_of(j), dst, me, place(j))

    def finish(stage, me, place, dst_of):
        for d in (1, 3, 2):
            j = (me + d) % 4
            arrived(stage, j, dst_of(j), place(j))

    loads = [
        pltpu.make_async_copy(shard_hbm, shard_ref, lsem.at[0]),
        pltpu.make_async_copy(weight_hbm, weight_ref, lsem.at[1]),
        pltpu.make_async_copy(cot_hbm, cot_t, lsem.at[2]),
        pltpu.make_async_copy(act_hbm, act_g.at[x], lsem.at[3]),
        pltpu.make_async_copy(bas_hbm, bas_g.at[x], lsem.at[4]),
    ]
    for cp in loads:
        cp.start()

    barrier = pltpu.get_barrier_semaphore()
    for me, place in ((x, at_x), (y, at_y), (zh, at_z), (col, at_c)):
        for d in (1, 2, 3):
            pl.semaphore_signal(barrier, inc=1, device_id=place((me + d) % 4), device_id_type=MESH)

    pl.semaphore_wait(barrier, 12)

    keep = pl.multiple_of(core * 224, 224)
    give = pl.multiple_of((1 - core) * 224, 224)
    sibling = at_c(col + 1 - 2 * core)
    partner = at_c((col + 2) % 4)
    send(S_H, 0, h_src.at[pl.ds(give, 224)], h_a, 0, sibling)
    start(S_ACT, x, at_x, lambda j: act_hbm, act_g.at[x])

    loads[0].wait()
    loads[1].wait()
    ids = jnp.transpose(jnp.broadcast_to(shard_ref[...].astype(F32), (128, 256)))
    lane = lax.broadcasted_iota(jnp.int32, (256, 128), 1).astype(F32)
    weight = jnp.zeros((256, 128), F32)
    for j in range(16):
        weight = weight + jnp.where(ids == lane + float(128 * j), weight_ref[j:j + 1, :], 0.0)
    weight = jnp.sum(weight, axis=1, keepdims=True)

    arrived(S_H, 0, h_a, sibling)
    h_a[...] = h_a[...] + h_src[pl.ds(keep, 224)]
    send(S_H, 1, h_a, h_b, 1, partner)
    loads[2].wait()
    cot[...] = (jnp.transpose(cot_t[...].astype(F32)) * weight).astype(BF16)
    arrived(S_H, 1, h_b, partner)
    h_win[pl.ds(keep, 224)] = h_a[...] + h_b[...]
    send(S_H, 2, h_win.at[pl.ds(keep, 224)], h_win.at[pl.ds(keep, 224)], 2, sibling)
    arrived(S_H, 2, h_win.at[pl.ds(give, 224)], sibling)

    for j in range(4):
        p_src[j] = jnp.dot(cot[...], h_win[:, 128 * j:128 * (j + 1)], preferred_element_type=F32).astype(BF16)
    start(S_PX, x, at_x, lambda j: p_src.at[j], p_x.at[x])

    e_x[x] = e_src[pl.ds(pl.multiple_of(128 * x, 128), 128)]
    start(S_EIX, x, at_x, lambda j: e_src.at[pl.ds(pl.multiple_of(128 * j, 128), 128)], e_x.at[x])

    finish(S_PX, x, at_x, lambda j: p_x.at[j])
    p_x[x] = p_src[x]
    start(S_BAS, x, at_x, lambda j: bas_hbm, bas_g.at[x])
    total = (p_x[0].astype(F32) + p_x[1].astype(F32)) + (p_x[2].astype(F32) + p_x[3].astype(F32))
    for j in range(4):
        p_y0[j] = total[64 * j:64 * (j + 1)].astype(BF16)
    start(S_PY, y, at_y, lambda j: p_y0.at[j], p_y.at[y])
    p_y[y] = p_y0[y]
    finish(S_PY, y, at_y, lambda j: p_y.at[j])
    p_z0[...] = ((p_y[0].astype(F32) + p_y[1].astype(F32)) + (p_y[2].astype(F32) + p_y[3].astype(F32))).astype(BF16)
    start(S_PZ, zh, at_z, lambda j: p_z0, p_z.at[zh])
    p_z[zh] = p_z0[...]
    finish(S_EIX, x, at_x, lambda j: e_x.at[j])
    start(S_EIC, col, at_c, lambda j: e_x.at[j], e_c.at[col])
    e_c[col] = e_x[col]
    finish(S_PZ, zh, at_z, lambda j: p_z.at[j])
    p_g[y] = ((p_z[0].astype(F32) + p_z[1].astype(F32)) + (p_z[2].astype(F32) + p_z[3].astype(F32))).astype(BF16)
    start(S_PG, y, at_y, lambda j: p_g.at[y], p_g.at[y])
    loads[3].wait()
    finish(S_ACT, x, at_x, lambda j: act_g.at[j])
    finish(S_PG, y, at_y, lambda j: p_g.at[j])

    pk = jnp.transpose(p_g[...].reshape(256, 128).astype(F32)).astype(BF16)
    for j in range(4):
        r_src[:, 128 * j:128 * (j + 1)] = jnp.dot(pk, act_g[j], preferred_element_type=F32).astype(BF16)

    diagonal = col == y

    @pl.when(jnp.logical_not(diagonal))
    def _():
        cp = pltpu.make_async_remote_copy(
            src_ref=r_src, dst_ref=r_c.at[col], send_sem=ssem.at[S_RC, 0], recv_sem=rsem.at[S_RC, col],
            device_id=at_c(y), device_id_type=MESH)
        cp.start()
        cp.wait_send()

    @pl.when(diagonal)
    def _():
        r_c[col] = r_src[...]
        finish(S_RC, col, at_c, lambda j: r_c.at[j])
        r_full[zh] = ((r_c[0].astype(F32) + r_c[1].astype(F32)) + (r_c[2].astype(F32) + r_c[3].astype(F32))).astype(BF16)
        cps = []
        for d in (2, 1, 3):
            j = (zh + d) % 4
            cp = pltpu.make_async_remote_copy(
                src_ref=r_full.at[zh], dst_ref=r_full.at[zh], send_sem=ssem.at[S_RZ, d], recv_sem=rsem.at[S_RZ, zh],
                device_id=at_z(j), device_id_type=MESH)
            cp.start()
            cps.append(cp)
        finish(S_RZ, zh, at_z, lambda j: r_full.at[j])
        for d in (2, 1, 3):
            j = (y + d) % 4
            cp = pltpu.make_async_remote_copy(
                src_ref=r_full, dst_ref=r_full, send_sem=ssem.at[S_RY, d], recv_sem=rsem.at[S_RY, 0],
                device_id=at_y(j), device_id_type=MESH)
            cp.start()
            cps.append(cp)
        for cp in cps:
            cp.wait_send()

    @pl.when(jnp.logical_not(diagonal))
    def _():
        arrived(S_RY, 0, r_full, at_y(col))

    loads[4].wait()
    finish(S_BAS, x, at_x, lambda j: bas_g.at[j])
    for j in range(4):
        acc = jnp.dot(r_full[0], bas_g[j, 0:512], preferred_element_type=F32)
        for z in range(1, 4):
            acc = acc + jnp.dot(r_full[z], bas_g[j, 512 * z:512 * (z + 1)], preferred_element_type=F32)
        t_src[j] = acc.astype(BF16)
    start(S_TC, col, at_c, lambda j: t_src.at[j], t_c.at[col])
    t_c[col] = t_src[col]
    finish(S_EIC, col, at_c, lambda j: e_c.at[j])
    damped = (e_c[0].astype(F32) + e_c[1].astype(F32)) + (e_c[2].astype(F32) + e_c[3].astype(F32)) + DAMPING
    finish(S_TC, col, at_c, lambda j: t_c.at[j])
    turned = (t_c[0].astype(F32) + t_c[1].astype(F32)) + (t_c[2].astype(F32) + t_c[3].astype(F32))
    c_all[col] = (turned / damped).astype(BF16)
    start(S_CC, col, at_c, lambda j: c_all.at[col], c_all.at[col])
    finish(S_CC, col, at_c, lambda j: c_all.at[j])

    for z in range(4):
        acc = None
        for j in range(4):
            term = lax.dot_general(
                c_all[j], bas_g[j, 512 * z:512 * (z + 1)], (((1,), (1,)), ((), ())), preferred_element_type=F32)
            acc = term if acc is None else acc + term
        acc = acc.astype(BF16)
        for j in range(4):
            q_src[j, z] = acc[32 * j:32 * (j + 1)]
    start(S_QY, y, at_y, lambda j: q_src.at[j], q_y.at[y])
    q_y[y] = q_src[y]
    finish(S_QY, y, at_y, lambda j: q_y.at[j])
    for z in range(4):
        q_z0[z] = ((q_y[0, z].astype(F32) + q_y[1, z].astype(F32)) + (q_y[2, z].astype(F32) + q_y[3, z].astype(F32))).astype(BF16)
    start(S_QZ, zh, at_z, lambda j: q_z0.at[j], q_z.at[zh])
    q_z[zh] = q_z0[zh]
    finish(S_QZ, zh, at_z, lambda j: q_z.at[j])
    piece = ((q_z[0].astype(F32) + q_z[1].astype(F32)) + (q_z[2].astype(F32) + q_z[3].astype(F32))).astype(BF16)
    ret[zh, 0, x, y] = piece[:, 0:256]
    ret[zh, 1, x, y] = piece[:, 256:512]

    start(S_GZ, zh, at_z, lambda j: ret.at[zh, :, x, y], ret.at[zh, :, x, y])
    finish(S_GZ, zh, at_z, lambda j: ret.at[j, :, x, y])
    start(S_GY0, y, at_y, lambda j: ret.at[:, 0, x, y], ret.at[:, 0, x, y])
    start(S_GX1, x, at_x, lambda j: ret.at[:, 1, x, y], ret.at[:, 1, x, y])
    finish(S_GY0, y, at_y, lambda j: ret.at[:, 0, x, j])
    start(S_GX0, x, at_x, lambda j: ret.at[:, 0, x], ret.at[:, 0, x])
    finish(S_GX1, x, at_x, lambda j: ret.at[:, 1, j, y])
    start(S_GY1, y, at_y, lambda j: ret.at[:, 1, :, y], ret.at[:, 1, :, y])
    outs = []
    for half in range(2):
        if half == 0:
            finish(S_GX0, x, at_x, lambda j: ret.at[:, 0, j])
        else:
            finish(S_GY1, y, at_y, lambda j: ret.at[:, 1, :, j])
        for z in range(4):
            rhs = ret[z, half].reshape(512, 256)
            n = half * 4 + z
            out_buf[n] = jnp.dot(h_win[...], rhs, preferred_element_type=F32).astype(BF16)
            at = 512 * z + 256 * half
            cp = pltpu.make_async_copy(out_buf.at[n], out_hbm.at[:, at:at + 256], osem.at[n])
            cp.start()
            outs.append(cp)
    for cp in sends:
        cp.wait_send()
    for cp in outs:
        cp.wait()


def per_device(cotangent, activations, shard_of_token, shard_weight, hidden_basis, input_basis, eigenvalues, panel_order):
    vmem = pl.BlockSpec(memory_space=pltpu.VMEM)
    hbm = pl.BlockSpec(memory_space=pltpu.HBM)

    def buf(*shape):
        return pltpu.VMEM(shape, BF16)

    h_src, e_src = pl.pallas_call(
        pick,
        out_shape=[jax.ShapeDtypeStruct((448, 512), BF16), jax.ShapeDtypeStruct((512, 128), BF16)],
        in_specs=[hbm, hbm, hbm],
        out_specs=[vmem, vmem],
        scratch_shapes=[pltpu.SMEM((2,), jnp.int32), pltpu.SemaphoreType.DMA((5,))],
        name="pick",
    )(panel_order, hidden_basis, eigenvalues)

    return pl.pallas_call(
        kernel,
        out_shape=jax.ShapeDtypeStruct((448, 2048), BF16),
        in_specs=[hbm, hbm, hbm, hbm, hbm, vmem, vmem],
        out_specs=hbm,
        scratch_shapes=[
            buf(448, 256), buf(256, 448), pltpu.VMEM((1, 256), jnp.int32), pltpu.VMEM((16, 128), F32),
            buf(4, 256, 128), buf(4, 2048, 128),
            buf(4, 128, 128), buf(4, 128, 128),
            buf(224, 512), buf(224, 512), buf(448, 512),
            buf(4, 256, 128), buf(4, 256, 128), buf(4, 64, 128), buf(4, 64, 128), buf(64, 128), buf(4, 64, 128), buf(4, 64, 128),
            buf(128, 512), buf(4, 128, 512), buf(4, 128, 512),
            buf(4, 128, 128), buf(4, 128, 128), buf(4, 128, 128),
            buf(4, 4, 32, 512), buf(4, 4, 32, 512), buf(4, 32, 512), buf(4, 32, 512), buf(4, 2, 4, 4, 32, 256),
            buf(8, 448, 256),
            pltpu.SemaphoreType.DMA((N_STAGES, 4)),
            pltpu.SemaphoreType.DMA((N_STAGES, 4)),
            pltpu.SemaphoreType.DMA((5,)),
            pltpu.SemaphoreType.DMA((8,)),
        ],
        compiler_params=pltpu.CompilerParams(
            collective_id=0, has_side_effects=True, vmem_limit_bytes=48 * 1024 * 1024),
        cost_estimate=pl.CostEstimate(flops=3_000_000_000, bytes_accessed=12_000_000, transcendentals=0),
        name="influence",
    )(
        cotangent.T, activations, shard_of_token.reshape(1, 256), shard_weight.reshape(16, 128),
        input_basis, h_src, e_src,
    )


def solution(mesh):
    placed = (
        P("col", "row"),
        P("col", "row"),
        P("col"),
        P(),
        P("row", "col"),
        P("col", "row"),
        P("col", "row"),
        P(),
    )
    return jax.shard_map(
        per_device, mesh=mesh, in_specs=placed, out_specs=P("row", "col"), check_vma=False
    )
```

time: 1140 us -> 114 us (0.10); the launches traced: 1130 us -> 113 us
  blocking collectives: 853 us -> 0 us
  waiting for transfers between devices: 226 us -> 0 us
  Pallas kernels: 0 us -> 110 us
  matrix products: 19.4 us -> 0 us
  between operations: 19 us -> 0.09 us
    psum x2 -> x0, blocking collectives: 853 us -> none  [the longest x1 428 us: per_device(): returned = lax.psum(return_term, 'row').astype(jnp.bfloat16)]
    pallas_call x0 -> x2, Pallas kernels: none -> 110 us  [the longest x1 108 us: per_device(): pl.pallas_call(kernel, out_shape=jax.ShapeDtypeStruct((448, 2048), BF16),...]
    all_gather x1 -> x0, waiting for transfers between devices: 104 us -> none  [per_device(): full_rows = lax.all_gather(activations, 'row', axis=1, tiled=True)]
    reduce_scatter x1 -> x0, waiting for transfers between devices: 68.2 us -> none  [per_device(): lax.psum_scatter(lax.dot_general(full_rows, scaled, (((0,), (0,)), ((), (...]
    psum x2 -> x0, waiting for transfers between devices: 53.5 us -> none  [the longest x1 53.5 us: per_device(): turned = lax.psum(turn_term.astype(jnp.bfloat16), 'col').astype(jnp.float32)]
    dot_general x5 -> x0, matrix products: 19.4 us -> none  [the longest x1 7.36 us: per_device(): lax.dot_general(full_rows, scaled, (((0,), (0,)), ((), ())), preferred_el...]
  transfers between devices with their start and end apart: 4 -> 0, of which waited for: 3 -> 0; matrix products, arithmetic and copies ran while one was open for 1% -> 0% of each run, Pallas kernels for 0% -> 0%
where the time goes in v1:
time: 114 us; the launch traced here: 113 us
  Pallas kernels  110 us (96%)
  local copies, waits for them, and re-layouts  3.17 us (3%)
    pallas_call x1, Pallas kernels, per_device(): pl.pallas_call(kernel, out_shape=jax.ShapeDtypeStruct((448, 2048), BF16),...  108 us
    unnamed x15, local copies, waits for them, and re-layouts  3.17 us

profile of v1, /device:TPU:6, one launch (start us, length us, event | category | flops | bytes accessed | tf_op | source)
XLA Modules:
  0.0 112.9 jit_solution(12951372574784147147)
XLA Ops:
  0.0 0.0 copy-start
  0.0 0.0 copy-start.2
  0.0 0.0 copy-start.4
  0.0 0.0 copy-start.5
  0.0 0.0 copy-start.6
  0.0 1.7 %pick.1 = (bf16[448,512]{1,0:T(8,128)(2,1)}, bf16[512,128]{1,0:T(8,128)(2,1)}) custom-call(s32[2]{0:T(128)} %order_hbm.1, bf16[448,7168]{1,0:T(8,128)(2,1)} %hid_hbm.1, bf16[7168,128]{1,0:T(8,128)(2,1)} %eig_hbm.1), custom_call_target="tpu_custom_call" | custom-call | tf_op jit(solution)/shard_map/pick/pallas_call | solution.py:299
  1.7 0.0 copy-done
  1.8 0.0 copy-done.2
  1.8 0.0 copy-done.4
  1.8 0.0 copy-done.5
  1.8 0.0 copy-done.6
  1.8 0.0 copy-start.1
  1.8 1.0 copy-done.1
  2.8 0.0 copy-start.3
  2.8 0.9 copy-done.3
  3.7 107.9 %influence.1 = bf16[448,2048]{1,0:T(8,128)(2,1)S(1)} custom-call(bf16[448,256]{1,0:T(8,128)(2,1)S(1)} %bitcast.3, bf16[256,128]{1,0:T(8,128)(2,1)S(1)} %copy-done.4, s32[1,256]{1,0:T(1,128)S(1)} %bitcast.5, f32[16,128]{1,0:T(8,128)S(1)} %bitcast.4, bf16[2048,128]{1,0:T(8,128)(2,1)S(1)} %copy-done, bf16[448,512]{1,0:T(8,128)(2,1)S(1)} %copy-done.1, ...), custom_call_target="tpu_custom_call" | custom-call | flops 3000000000 | bytes 12000000 | tf_op jit(solution)/shard_map/influence/pallas_call | solution.py:308
  111.7 1.2 %copy.10 = bf16[448,2048]{1,0:T(8,128)(2,1)} copy(bf16[448,2048]{1,0:T(8,128)(2,1)S(1)} %influence.1) | data formatting | bytes 3670016
Async XLA Ops:
  0.0 1.7 %copy-start = (bf16[2048,128]{1,0:T(8,128)(2,1)S(1)}, bf16[2048,128]{1,0:T(8,128)(2,1)}, u32[]{:S(2)}) copy-start(bf16[2048,128]{1,0:T(8,128)(2,1)} %bas_hbm.1) | copy-start | bytes 1572868
  0.0 1.8 %copy-start.2 = (bf16[256,448]{0,1:T(8,128)(2,1)S(1)}, bf16[256,448]{0,1:T(8,128)(2,1)}, u32[]{:S(2)}) copy-start(bf16[256,448]{0,1:T(8,128)(2,1)} %param.8) | copy-start | bytes 688132
  0.0 1.8 %copy-start.4 = (bf16[256,128]{1,0:T(8,128)(2,1)S(1)}, bf16[256,128]{1,0:T(8,128)(2,1)}, u32[]{:S(2)}) copy-start(bf16[256,128]{1,0:T(8,128)(2,1)} %act_hbm.1) | copy-start | bytes 196612
  0.0 1.8 %copy-start.5 = (f32[2048]{0:T(1024)S(1)}, f32[2048]{0:T(1024)}, u32[]{:S(2)}) copy-start(f32[2048]{0:T(1024)} %param.11) | copy-start | bytes 24580
  0.0 1.8 %copy-start.6 = (s32[256]{0:T(256)S(1)}, s32[256]{0:T(256)}, u32[]{:S(2)}) copy-start(s32[256]{0:T(256)} %param.10) | copy-start | bytes 3076
  1.8 1.0 copy-start.1
  2.8 0.9 copy-start.3

commit v2 on v0

v2 whole, which is shorter than its diff:
```python
import jax
import jax.numpy as jnp
from jax import lax
from jax.experimental import pallas as pl
from jax.experimental.pallas import tpu as pltpu
from jax.sharding import PartitionSpec as P

PANEL = 256
LAST = 111
PER_COL = 28
DAMPING = 0.01
MESH = pl.DeviceIdType.MESH
F32 = jnp.float32
BF16 = jnp.bfloat16

(R_TURN, R_ACT, R_ASIB, R_BAS, R_SIB, R_EIX, R_EIC, R_H, R_HL, R_PY, R_PX, R_PZ, R_PG, R_RY, R_RZ, R_RG, R_TC, R_QY, R_QZ,
 R_GZ, R_GX, R_GY, R_FX, R_FY) = (
    0, 1, 5, 9, 13, 17, 21, 25, 28, 30, 38, 42, 46, 50, 54, 58, 74, 75, 91, 95, 103, 107, 111, 127)
N_RECV = 143
N_SEND = 144


def pick(order_hbm, hid_hbm, eig_hbm, h_src, e_src, order, sems):
    col = lax.axis_index("col")
    cp = pltpu.make_async_copy(order_hbm, order, sems.at[0])
    cp.start()
    cp.wait()
    other = order[0] + order[1] - LAST
    place = pl.multiple_of((other - col * PER_COL) * PANEL, PANEL)
    mine = (other >= col * PER_COL) & (other < (col + 1) * PER_COL)
    end = (PER_COL - 1) * PANEL

    def fetch(have, at, k):
        h_part = h_src.at[k]
        e_part = e_src.at[PANEL * k:PANEL * (k + 1)]

        def copies():
            return (pltpu.make_async_copy(hid_hbm.at[:, pl.ds(at, PANEL)], h_part, sems.at[1 + 2 * k]),
                    pltpu.make_async_copy(eig_hbm.at[pl.ds(at, PANEL)], e_part, sems.at[2 + 2 * k]))

        @pl.when(have)
        def _():
            for cp in copies():
                cp.start()

        @pl.when(jnp.logical_not(have))
        def _():
            h_part[...] = jnp.zeros(h_part.shape, BF16)
            e_part[...] = jnp.zeros(e_part.shape, BF16)

        def settle():
            @pl.when(have)
            def _():
                for cp in copies():
                    cp.wait()
        return settle

    settle = [fetch(mine, place, 0), fetch(col == 3, end, 1)]
    for wait in settle:
        wait()


def add4(a, b, c, d):
    return (a.astype(F32) + b.astype(F32)) + (c.astype(F32) + d.astype(F32))


def kernel(
    cot_hbm, act_hbm, shard_hbm, weight_hbm, bas_hbm, h_src, e_src, out_ref,
    cot_t, cot, shard_ref, weight_ref, act_g, bas_g,
    e_x, e_c,
    h_a, h_b, h_win,
    p_src, p_y, p_x0, p_x, p_z0, p_z, p_s, p_g,
    pk, r_src, r_y, r_full,
    t_src, t_in, c_all,
    q_src, q_y, q_z0, q_z, g_src, ret,
    ssem, rsem, lsem,
):
    row = lax.axis_index("row")
    col = lax.axis_index("col")
    x = row % 4
    zh = (row // 4) % 4
    y = row // 16
    core = col % 2
    zlo = col // 2

    def at_x(j):
        return (y * 16 + zh * 4 + j, col)

    def at_y(j):
        return (j * 16 + zh * 4 + x, col)

    def at_z(j):
        return (y * 16 + j * 4 + x, col)

    def at_c(j):
        return (row, j)

    def at_yc(j, k):
        return (j * 16 + zh * 4 + x, k)

    sibling = at_c(zlo * 2 + 1 - core)
    partner = at_c((col + 2) % 4)

    sends = []
    used = [0]

    def copy(src, dst, recv, device):
        cp = pltpu.make_async_remote_copy(
            src_ref=src, dst_ref=dst, send_sem=ssem.at[used[0]], recv_sem=rsem.at[recv],
            device_id=device, device_id_type=MESH)
        used[0] += 1
        cp.start()
        return cp

    def send(src, dst, recv, device):
        sends.append(copy(src, dst, recv, device))

    def arrived(recv, dst):
        pltpu.make_async_remote_copy(
            src_ref=dst, dst_ref=dst, send_sem=ssem.at[0], recv_sem=rsem.at[recv],
            device_id=sibling, device_id_type=MESH).wait_recv()

    def start(base, me, place, src_of, dst):
        for d in (2, 1, 3):
            j = (me + d) % 4
            send(src_of(j), dst, base + me, place(j))

    def finish(base, me, dst_of):
        for d in (1, 3, 2):
            j = (me + d) % 4
            arrived(base + j, dst_of(j))

    barrier = pltpu.get_barrier_semaphore()
    for d in (1, 2, 3):
        pl.semaphore_signal(barrier, inc=1, device_id=at_c((col + d) % 4), device_id_type=MESH)
    for me, place in ((x, at_x), (y, at_y), (zh, at_z)):
        for d in (2, 1, 3):
            pl.semaphore_signal(barrier, inc=1, device_id=place((me + d) % 4), device_id_type=MESH)
    for d in (2, 1, 3):
        pl.semaphore_signal(
            barrier, inc=1, device_id=(at_z((zh + d) % 4)[0], zlo * 2 + 1 - core), device_id_type=MESH)


    @pl.when(col != y)
    def _():
        for d in (2, 1, 3):
            pl.semaphore_signal(barrier, inc=1, device_id=at_yc((y + d) % 4, y), device_id_type=MESH)

    loads = [
        pltpu.make_async_copy(shard_hbm, shard_ref, lsem.at[0]),
        pltpu.make_async_copy(weight_hbm, weight_ref, lsem.at[1]),
        pltpu.make_async_copy(cot_hbm, cot_t, lsem.at[2]),
        pltpu.make_async_copy(bas_hbm, bas_g.at[core, x], lsem.at[3]),
    ]
    for cp in loads:
        cp.start()

    pl.semaphore_wait(barrier, jnp.where(col == y, 15, 18))

    keep = pl.multiple_of(core * 224, 224)
    give = pl.multiple_of((1 - core) * 224, 224)
    holder = col == 3

    def last_copies(n):
        return [pltpu.make_async_remote_copy(
            src_ref=src, dst_ref=src_to, send_sem=ssem.at[n + i], recv_sem=rsem.at[R_HL],
            device_id=at_c(k), device_id_type=MESH)
            for i, (src, src_to, k) in enumerate((
                (h_src.at[1, 0:224], h_win.at[1, 0:224], 0),
                (h_src.at[1, 224:448], h_win.at[1, 224:448], 1),
                (h_src.at[1], h_win.at[1], 2)))]

    first_last = used[0]
    used[0] += 3

    @pl.when(holder)
    def _():
        for cp in last_copies(first_last):
            cp.start()
        cp = pltpu.make_async_copy(h_src.at[1], h_win.at[1], lsem.at[5])
        cp.start()
        cp.wait()

    send(h_src.at[0, pl.ds(give, 224)], h_a, R_H, sibling)

    swap = used[0]

    @pl.when(col != y)
    def _():
        copy(act_hbm, act_g.at[y % 2, x], R_TURN, at_yc(col, y))

    @pl.when(col == y)
    def _():
        cp = pltpu.make_async_copy(act_hbm, act_g.at[core, x], lsem.at[4])
        cp.start()
        cp.wait()

    loads[0].wait()
    loads[1].wait()
    ids = jnp.transpose(jnp.broadcast_to(shard_ref[...].astype(F32), (128, 256)))
    lane = lax.broadcasted_iota(jnp.int32, (256, 128), 1).astype(F32)
    weight = jnp.zeros((256, 128), F32)
    for j in range(16):
        weight = weight + jnp.where(ids == lane + float(128 * j), weight_ref[j:j + 1, :], 0.0)
    weight = jnp.sum(weight, axis=1, keepdims=True)

    arrived(R_H, h_a)
    h_a[...] = h_a[...] + h_src[0, pl.ds(keep, 224)]
    send(h_a, h_b, R_H + 1, partner)
    x_up, x_down, x_far = (x + 1) % 4, (x + 3) % 4, (x + 2) % 4
    send(bas_hbm, bas_g.at[core, x], R_BAS + 0, at_x(x_up))
    send(bas_hbm, bas_g.at[core, x], R_BAS + 1, at_x(x_down))
    loads[2].wait()
    cot[...] = (jnp.transpose(cot_t[...].astype(F32)) * weight).astype(BF16)

    def project(p):
        part = jnp.dot(cot[...], h_win[p], preferred_element_type=F32).astype(BF16)
        for j in range(4):
            p_src[p, j] = part[64 * j:64 * (j + 1)]
        start(R_PY + 4 * p, y, at_y, lambda j: p_src.at[p, j], p_y.at[p, y])
        p_y[p, y] = p_src[p, y]

    @pl.when(zlo == 0)
    def _():
        arrived(R_HL, h_win.at[1, pl.ds(keep, 224)])
        cp = copy(h_win.at[1, pl.ds(keep, 224)], h_win.at[1, pl.ds(keep, 224)], R_HL + 1, sibling)
        arrived(R_HL + 1, h_win.at[1, pl.ds(give, 224)])
        cp.wait_send()

    @pl.when(col == 2)
    def _():
        arrived(R_HL, h_win.at[1])

    project(1)
    arrived(R_H + 1, h_b)
    h_win[0, pl.ds(keep, 224)] = h_a[...] + h_b[...]
    send(h_win.at[0, pl.ds(keep, 224)], h_win.at[0, pl.ds(keep, 224)], R_H + 2, sibling)

    @pl.when(col != y)
    def _():
        arrived(R_TURN, act_g.at[core, x])
    start(R_ACT, x, at_x, lambda j: act_g.at[core, x], act_g.at[core, x])
    send(act_g.at[core, x], act_g.at[core, x], R_ASIB + x, sibling)

    arrived(R_H + 2, h_win.at[0, pl.ds(give, 224)])
    project(0)

    @pl.when(holder)
    def _():
        for cp in last_copies(first_last):
            cp.wait_send()

    for p in (1, 0):
        finish(R_PY + 4 * p, y, lambda j: p_y.at[p, j])
        total = add4(p_y[p, 0], p_y[p, 1], p_y[p, 2], p_y[p, 3]).astype(BF16)
        for j in range(2):
            p_x0[2 * p + j] = total[:, 128 * j:128 * (j + 1)]
    start(R_PX, x, at_x, lambda j: p_x0.at[j], p_x.at[x])
    p_x[x] = p_x0[x]
    e_x[x] = e_src[pl.ds(pl.multiple_of(128 * x, 128), 128)]
    start(R_EIX, x, at_x, lambda j: e_src.at[pl.ds(pl.multiple_of(128 * j, 128), 128)], e_x.at[x])
    finish(R_PX, x, lambda j: p_x.at[j])
    p_z0[...] = add4(p_x[0], p_x[1], p_x[2], p_x[3]).astype(BF16)
    start(R_PZ, zh, at_z, lambda j: p_z0, p_z.at[zh])
    p_z[zh] = p_z0[...]
    for d in (1, 3, 2):
        j = (x + d) % 4
        arrived(R_ACT + j, act_g.at[core, j])
        send(act_g.at[core, j], act_g.at[core, j], R_ASIB + j, sibling)

    arrived(R_BAS + 0, bas_g.at[core, x_down])
    send(bas_g.at[core, x_down, 0:1024], bas_g.at[core, x_down, 0:1024], R_BAS + 2, at_x(x_up))
    arrived(R_BAS + 1, bas_g.at[core, x_up])
    send(bas_g.at[core, x_up, 1024:2048], bas_g.at[core, x_up, 1024:2048], R_BAS + 3, at_x(x_down))

    finish(R_PZ, zh, lambda j: p_z.at[j])
    p_s[...] = add4(p_z[0], p_z[1], p_z[2], p_z[3]).astype(BF16)
    first_turn = used[0]
    used[0] += 4

    def turn(k):
        return pltpu.make_async_remote_copy(
            src_ref=p_s, dst_ref=p_g.at[y], send_sem=ssem.at[first_turn + k], recv_sem=rsem.at[R_PG + y],
            device_id=at_yc(col, k), device_id_type=MESH)

    for k in range(4):
        away = (col != y) | (col != k)

        @pl.when(away)
        def _():
            turn(k).start()

        @pl.when(jnp.logical_not(away))
        def _():
            p_g[y] = p_s[...]

    finish(R_EIX, x, lambda j: e_x.at[j])
    for d in (2, 1, 3):
        j = (col + d) % 4
        half = pl.ds(pl.multiple_of(64 * (j % 2), 64), 64)
        send(e_x.at[:, half], e_c.at[col], R_EIC + col, at_c(j))
    e_c[col] = e_x[:, pl.ds(pl.multiple_of(64 * core, 64), 64)]
    for j in range(4):
        arrived(R_ASIB + j, act_g.at[1 - core, j])
    for j in range(4):
        @pl.when((col != y) | (j != y))
        def _():
            arrived(R_PG + j, p_g.at[j])

    turned_p = jnp.transpose(p_g[...].reshape(256, 128).astype(F32)).astype(BF16)
    pk[0] = turned_p[0:64]
    pk[1] = turned_p[64:128]
    mine = pk[core]
    for q in range(2):
        for j in range(4):
            part = jnp.dot(mine, act_g[q, j], preferred_element_type=F32).astype(BF16)
            for k in range(4):
                r_src[k, q, :, 128 * j:128 * (j + 1)] = part[16 * k:16 * (k + 1)]
    start(R_RY, y, at_y, lambda j: r_src.at[j], r_y.at[y])
    r_y[y] = r_src[y]
    send(bas_hbm, bas_g.at[core, x], R_SIB + 0, sibling)
    send(bas_g.at[core, x_down], bas_g.at[core, x_down], R_SIB + 1, sibling)
    send(bas_g.at[core, x_up], bas_g.at[core, x_up], R_SIB + 2, sibling)
    finish(R_RY, y, lambda j: r_y.at[j])
    here = pl.ds(pl.multiple_of(16 * y, 16), 16)
    r_full[zh, :, here] = add4(r_y[0], r_y[1], r_y[2], r_y[3]).astype(BF16)
    start(R_RZ, zh, at_z, lambda j: r_full.at[zh, :, here], r_full.at[zh, :, here])
    start(R_RG + 4 * zh, y, at_y, lambda j: r_full.at[zh, :, here], r_full.at[zh, :, here])
    arrived(R_BAS + 2, bas_g.at[core, x_far, 0:1024])
    arrived(R_BAS + 3, bas_g.at[core, x_far, 1024:2048])
    send(bas_g.at[core, x_far], bas_g.at[core, x_far], R_SIB + 3, sibling)
    for d in (1, 3, 2):
        z = (zh + d) % 4
        arrived(R_RZ + z, r_full.at[z, :, here])
        start(R_RG + 4 * z, y, at_y, lambda j: r_full.at[z, :, here], r_full.at[z, :, here])
    for d in (0, 1, 3, 2):
        z = (zh + d) % 4
        for e in (1, 3, 2):
            j = (y + e) % 4
            arrived(R_RG + 4 * z + j, r_full.at[z, :, pl.ds(pl.multiple_of(16 * j, 16), 16)])

    for k in range(4):
        @pl.when((col != y) | (col != k))
        def _():
            turn(k).wait_send()

    loads[3].wait()
    for j, slot in ((0, x), (1, x_down), (2, x_up), (3, x_far)):
        arrived(R_SIB + j, bas_g.at[1 - core, slot])
    own = []
    for j in range(4):
        acc = None
        for q in range(2):
            for z in range(4):
                term = jnp.dot(r_full[z, q], bas_g[q, j, 512 * z:512 * (z + 1)], preferred_element_type=F32)
                acc = term if acc is None else acc + term
        own.append(acc)
        t_src[j] = acc.astype(BF16)
    send(t_src, t_in, R_TC, partner)
    finish(R_EIC, col, lambda j: e_c.at[j])
    damped = add4(e_c[0], e_c[1], e_c[2], e_c[3]) + DAMPING
    arrived(R_TC, t_in)
    for j in range(4):
        c_all[j] = ((own[j] + t_in[j].astype(F32)) / damped[j]).astype(BF16)

    z_order = [(zh + d) % 4 for d in (2, 1, 3, 0)]
    for z in z_order:
        for q in range(2):
            acc = None
            for j in range(4):
                term = lax.dot_general(
                    c_all[j], bas_g[q, j, pl.ds(pl.multiple_of(512 * z, 512), 512)], (((1,), (1,)), ((), ())),
                    preferred_element_type=F32)
                acc = term if acc is None else acc + term
            acc = acc.astype(BF16)
            for j in range(4):
                q_src[j, z, q] = acc[16 * j:16 * (j + 1)]
        for d in (2, 1, 3):
            j = (y + d) % 4
            send(q_src.at[j, z], q_y.at[y, z], R_QY + 4 * y + z, at_y(j))
        q_y[y, z] = q_src[y, z]
    for n, z in enumerate(z_order):
        for d in (1, 3, 2):
            j = (y + d) % 4
            arrived(R_QY + 4 * j + z, q_y.at[j, z])
        total = add4(q_y[0, z], q_y[1, z], q_y[2, z], q_y[3, z]).astype(BF16)
        if n < 3:
            q_z0[z] = total
            send(q_z0.at[z], q_z.at[zh], R_QZ + zh, at_z(z))
        else:
            q_z[zh] = total
    finish(R_QZ, zh, lambda j: q_z.at[j])
    piece = add4(q_z[0], q_z[1], q_z[2], q_z[3]).astype(BF16)

    for half in range(2):
        g_src[:, half] = piece[:, :, 256 * half:256 * (half + 1)]
    ret[zh, :, x, core, y] = g_src[core]
    for d in (2, 1, 3):
        j = (zh + d) % 4
        for k in (core, 1 - core):
            send(g_src.at[k], ret.at[zh, :, x, core, y], R_GZ + 2 * zh + core, (at_z(j)[0], zlo * 2 + k))
    send(g_src.at[1 - core], ret.at[zh, :, x, core, y], R_GZ + 2 * zh + core, sibling)
    arrived(R_GZ + 2 * zh + 1 - core, ret.at[zh, :, x, 1 - core, y])
    for d in (1, 3, 2):
        j = (zh + d) % 4
        for k in range(2):
            arrived(R_GZ + 2 * j + k, ret.at[j, :, x, k, y])

    start(R_GX, x, at_x, lambda j: ret.at[:, :, x, :, y], ret.at[:, :, x, :, y])
    start(R_GY, y, at_y, lambda j: ret.at[:, :, x, :, y], ret.at[:, :, x, :, y])
    for d in (1, 3, 2):
        j = (y + d) % 4
        arrived(R_GY + j, ret.at[:, :, x, :, j])
        for e in (2, 1, 3):
            send(ret.at[:, 0, x, :, j], ret.at[:, 0, x, :, j], R_FX + 4 * x + j, at_x((x + e) % 4))
        j = (x + d) % 4
        arrived(R_GX + j, ret.at[:, :, j, :, y])
        for e in (2, 1, 3):
            send(ret.at[:, 1, j, :, y], ret.at[:, 1, j, :, y], R_FY + 4 * j + y, at_y((y + e) % 4))
    for half in range(2):
        for d in (1, 3, 2):
            for e in (1, 3, 2):
                jx, jy = (x + e) % 4, (y + d) % 4
                arrived((R_FX if half == 0 else R_FY) + 4 * jx + jy, ret.at[:, half, jx, :, jy])
        for z in range(4):
            acc = jnp.dot(h_win[0], ret[z, half, 0:2].reshape(256, 256), preferred_element_type=F32)
            acc = acc + jnp.dot(h_win[1], ret[z, half, 2:4].reshape(256, 256), preferred_element_type=F32)
            at = 512 * z + 256 * half
            out_ref[:, at:at + 256] = acc.astype(BF16)
    for cp in sends:
        cp.wait_send()

    @pl.when(col != y)
    def _():
        pltpu.make_async_remote_copy(
            src_ref=act_hbm, dst_ref=act_g.at[y % 2, x], send_sem=ssem.at[swap], recv_sem=rsem.at[R_TURN],
            device_id=at_yc(col, y), device_id_type=MESH).wait_send()


def per_device(cotangent, activations, shard_of_token, shard_weight, hidden_basis, input_basis, eigenvalues, panel_order):
    vmem = pl.BlockSpec(memory_space=pltpu.VMEM)
    hbm = pl.BlockSpec(memory_space=pltpu.HBM)

    def buf(*shape):
        return pltpu.VMEM(shape, BF16)

    h_src, e_src = pl.pallas_call(
        pick,
        out_shape=[jax.ShapeDtypeStruct((2, 448, 256), BF16), jax.ShapeDtypeStruct((512, 128), BF16)],
        in_specs=[hbm, hbm, hbm],
        out_specs=[vmem, vmem],
        scratch_shapes=[pltpu.SMEM((2,), jnp.int32), pltpu.SemaphoreType.DMA((5,))],
        compiler_params=pltpu.CompilerParams(vmem_limit_bytes=60 * 1024 * 1024),
        name="pick",
    )(panel_order, hidden_basis, eigenvalues)

    return pl.pallas_call(
        kernel,
        out_shape=jax.ShapeDtypeStruct((448, 2048), BF16),
        in_specs=[hbm, hbm, hbm, hbm, hbm, vmem, vmem],
        out_specs=vmem,
        scratch_shapes=[
            buf(448, 256), buf(256, 448), pltpu.VMEM((1, 256), jnp.int32), pltpu.VMEM((16, 128), F32),
            buf(2, 4, 256, 128), buf(2, 4, 2048, 128),
            buf(4, 128, 128), buf(4, 4, 64, 128),
            buf(224, 256), buf(224, 256), buf(2, 448, 256),
            buf(2, 4, 64, 256), buf(2, 4, 64, 256), buf(4, 64, 128), buf(4, 64, 128), buf(64, 128), buf(4, 64, 128),
            buf(64, 128), buf(4, 64, 128),
            buf(2, 64, 256), buf(4, 2, 16, 512), buf(4, 2, 16, 512), buf(4, 2, 64, 512),
            buf(4, 64, 128), buf(4, 64, 128), buf(4, 64, 128),
            buf(4, 4, 2, 16, 512), buf(4, 4, 2, 16, 512), buf(4, 2, 16, 512), buf(4, 2, 16, 512), buf(2, 2, 16, 256),
            buf(4, 2, 4, 2, 4, 16, 256),
            pltpu.SemaphoreType.DMA((N_SEND,)),
            pltpu.SemaphoreType.DMA((N_RECV,)),
            pltpu.SemaphoreType.DMA((6,)),
        ],
        compiler_params=pltpu.CompilerParams(
            collective_id=0, has_side_effects=True, vmem_limit_bytes=60 * 1024 * 1024),
        cost_estimate=pl.CostEstimate(flops=3_000_000_000, bytes_accessed=12_000_000, transcendentals=0),
        name="influence",
    )(
        cotangent.T, activations, shard_of_token.reshape(1, 256), shard_weight.reshape(16, 128),
        input_basis, h_src, e_src,
    )


def solution(mesh):
    placed = (
        P("col", "row"),
        P("col", "row"),
        P("col"),
        P(),
        P("row", "col"),
        P("col", "row"),
        P("col", "row"),
        P(),
    )
    return jax.shard_map(
        per_device, mesh=mesh, in_specs=placed, out_specs=P("row", "col"), check_vma=False
    )
```

time: 1140 us -> 103 us (0.09)
  the two profiles are of different devices: /device:TPU:6 before, /device:TPU:1 now
where the time goes in v2:
time: 103 us; the launch traced here: 102 us
  Pallas kernels  99.5 us (97%)
  local copies, waits for them, and re-layouts  2.94 us (3%)
    pallas_call x1, Pallas kernels, per_device(): pl.pallas_call(kernel, out_shape=jax.ShapeDtypeStruct((448, 2048), BF16),...  97.9 us
    unnamed x1, local copies, waits for them, and re-layouts  2.94 us

profile of v2, /device:TPU:1, one launch (start us, length us, event | category | flops | bytes accessed | tf_op | source)
XLA Modules:
  0.0 102.4 jit_solution(12116672644543999082)
XLA Ops:
  0.0 1.6 %pick.1 = (bf16[2,448,256]{2,1,0:T(8,128)(2,1)}, bf16[512,128]{1,0:T(8,128)(2,1)}) custom-call(s32[2]{0:T(128)} %order_hbm.1, bf16[448,7168]{1,0:T(8,128)(2,1)} %hid_hbm.1, bf16[7168,128]{1,0:T(8,128)(2,1)} %eig_hbm.1), custom_call_target="tpu_custom_call" | custom-call | tf_op jit(solution)/shard_map/pick/pallas_call | solution.py:447
  1.6 97.9 %influence.1 = bf16[448,2048]{1,0:T(8,128)(2,1)} custom-call(bf16[448,256]{1,0:T(8,128)(2,1)} %bitcast.3, bf16[256,128]{1,0:T(8,128)(2,1)} %act_hbm.1, s32[1,256]{1,0:T(1,128)} %bitcast.5, f32[16,128]{1,0:T(8,128)} %bitcast.4, bf16[2048,128]{1,0:T(8,128)(2,1)} %bas_hbm.1, bf16[2,448,256]{2,1,0:T(8,128)(2,1)} %get-tuple-element.7.h_src, ...), custom_call_target="tpu_custom_call" | custom-call | flops 3000000000 | bytes 12000000 | tf_op jit(solution)/shard_map/influence/pallas_call | solution.py:457
  99.5 2.9 %copy.10 = bf16[448,2048]{1,0:T(8,128)(2,1)} copy(bf16[448,2048]{1,0:T(8,128)(2,1)} %influence.1) | data formatting | bytes 3670016

commit v3 on v2

--- a/solution.py
+++ b/solution.py
@@ -15,9 +15,9 @@
 
 (R_TURN, R_ACT, R_ASIB, R_BAS, R_SIB, R_EIX, R_EIC, R_H, R_HL, R_PY, R_PX, R_PZ, R_PG, R_RY, R_RZ, R_RG, R_TC, R_QY, R_QZ,
  R_GZ, R_GX, R_GY, R_FX, R_FY) = (
-    0, 1, 5, 9, 13, 17, 21, 25, 28, 30, 38, 42, 46, 50, 54, 58, 74, 75, 91, 95, 103, 107, 111, 127)
-N_RECV = 143
-N_SEND = 144
+    0, 1, 5, 9, 15, 19, 23, 27, 30, 32, 40, 44, 48, 52, 56, 60, 76, 77, 93, 97, 105, 109, 113, 125)
+N_RECV = 137
+N_SEND = 160
 
 
 def pick(order_hbm, hid_hbm, eig_hbm, h_src, e_src, order, sems):
@@ -65,14 +65,14 @@
 
 
 def kernel(
-    cot_hbm, act_hbm, shard_hbm, weight_hbm, bas_hbm, h_src, e_src, out_ref,
+    cot_hbm, act_hbm, shard_hbm, weight_hbm, bas_hbm, h_src, e_src, ret, win_out,
     cot_t, cot, shard_ref, weight_ref, act_g, bas_g,
     e_x, e_c,
-    h_a, h_b, h_win,
+    h_keep, h_a, h_b, h_win,
     p_src, p_y, p_x0, p_x, p_z0, p_z, p_s, p_g,
     pk, r_src, r_y, r_full,
     t_src, t_in, c_all,
-    q_src, q_y, q_z0, q_z, g_src, ret,
+    q_src, q_y, q_z0, q_z, g_src,
     ssem, rsem, lsem,
 ):
     row = lax.axis_index("row")
@@ -146,19 +146,21 @@
         for d in (2, 1, 3):
             pl.semaphore_signal(barrier, inc=1, device_id=at_yc((y + d) % 4, y), device_id_type=MESH)
 
+    keep = pl.multiple_of(core * 224, 224)
+    give = pl.multiple_of((1 - core) * 224, 224)
     loads = [
         pltpu.make_async_copy(shard_hbm, shard_ref, lsem.at[0]),
         pltpu.make_async_copy(weight_hbm, weight_ref, lsem.at[1]),
         pltpu.make_async_copy(cot_hbm, cot_t, lsem.at[2]),
         pltpu.make_async_copy(bas_hbm, bas_g.at[core, x], lsem.at[3]),
+        pltpu.make_async_copy(h_src.at[0, pl.ds(keep, 224)], h_keep, lsem.at[4]),
+        pltpu.make_async_copy(e_src.at[pl.ds(pl.multiple_of(128 * x, 128), 128)], e_x.at[x], lsem.at[5]),
     ]
     for cp in loads:
         cp.start()
 
     pl.semaphore_wait(barrier, jnp.where(col == y, 15, 18))
 
-    keep = pl.multiple_of(core * 224, 224)
-    give = pl.multiple_of((1 - core) * 224, 224)
     holder = col == 3
 
     def last_copies(n):
@@ -177,7 +179,7 @@
     def _():
         for cp in last_copies(first_last):
             cp.start()
-        cp = pltpu.make_async_copy(h_src.at[1], h_win.at[1], lsem.at[5])
+        cp = pltpu.make_async_copy(h_src.at[1], h_win.at[1], lsem.at[7])
         cp.start()
         cp.wait()
 
@@ -191,7 +193,7 @@
 
     @pl.when(col == y)
     def _():
-        cp = pltpu.make_async_copy(act_hbm, act_g.at[core, x], lsem.at[4])
+        cp = pltpu.make_async_copy(act_hbm, act_g.at[core, x], lsem.at[6])
         cp.start()
         cp.wait()
 
@@ -205,11 +207,10 @@
     weight = jnp.sum(weight, axis=1, keepdims=True)
 
     arrived(R_H, h_a)
-    h_a[...] = h_a[...] + h_src[0, pl.ds(keep, 224)]
+    loads[4].wait()
+    h_a[...] = h_a[...] + h_keep[...]
     send(h_a, h_b, R_H + 1, partner)
     x_up, x_down, x_far = (x + 1) % 4, (x + 3) % 4, (x + 2) % 4
-    send(bas_hbm, bas_g.at[core, x], R_BAS + 0, at_x(x_up))
-    send(bas_hbm, bas_g.at[core, x], R_BAS + 1, at_x(x_down))
     loads[2].wait()
     cot[...] = (jnp.transpose(cot_t[...].astype(F32)) * weight).astype(BF16)
 
@@ -244,6 +245,9 @@
 
     arrived(R_H + 2, h_win.at[0, pl.ds(give, 224)])
     project(0)
+    wins = [pltpu.make_async_copy(h_win.at[p], win_out.at[:, PANEL * p:PANEL * (p + 1)], lsem.at[9 + p]) for p in range(2)]
+    for cp in wins:
+        cp.start()
 
     @pl.when(holder)
     def _():
@@ -257,9 +261,17 @@
             p_x0[2 * p + j] = total[:, 128 * j:128 * (j + 1)]
     start(R_PX, x, at_x, lambda j: p_x0.at[j], p_x.at[x])
     p_x[x] = p_x0[x]
-    e_x[x] = e_src[pl.ds(pl.multiple_of(128 * x, 128), 128)]
     start(R_EIX, x, at_x, lambda j: e_src.at[pl.ds(pl.multiple_of(128 * j, 128), 128)], e_x.at[x])
     finish(R_PX, x, lambda j: p_x.at[j])
+
+    low, high = pl.ds(0, 1024), pl.ds(1024, 1024)
+
+    def basis(slot, part, recv, j):
+        send(bas_g.at[core, slot, part], bas_g.at[core, slot, part], recv, at_x(j))
+
+    loads[3].wait()
+    basis(x, low, R_BAS + 0, x_up)
+    basis(x, high, R_BAS + 1, x_down)
     p_z0[...] = add4(p_x[0], p_x[1], p_x[2], p_x[3]).astype(BF16)
     start(R_PZ, zh, at_z, lambda j: p_z0, p_z.at[zh])
     p_z[zh] = p_z0[...]
@@ -268,10 +280,8 @@
         arrived(R_ACT + j, act_g.at[core, j])
         send(act_g.at[core, j], act_g.at[core, j], R_ASIB + j, sibling)
 
-    arrived(R_BAS + 0, bas_g.at[core, x_down])
-    send(bas_g.at[core, x_down, 0:1024], bas_g.at[core, x_down, 0:1024], R_BAS + 2, at_x(x_up))
-    arrived(R_BAS + 1, bas_g.at[core, x_up])
-    send(bas_g.at[core, x_up, 1024:2048], bas_g.at[core, x_up, 1024:2048], R_BAS + 3, at_x(x_down))
+    basis(x, high, R_BAS + 2, x_up)
+    basis(x, low, R_BAS + 3, x_down)
 
     finish(R_PZ, zh, lambda j: p_z.at[j])
     p_s[...] = add4(p_z[0], p_z[1], p_z[2], p_z[3]).astype(BF16)
@@ -294,6 +304,7 @@
         def _():
             p_g[y] = p_s[...]
 
+    loads[5].wait()
     finish(R_EIX, x, lambda j: e_x.at[j])
     for d in (2, 1, 3):
         j = (col + d) % 4
@@ -318,21 +329,27 @@
                 r_src[k, q, :, 128 * j:128 * (j + 1)] = part[16 * k:16 * (k + 1)]
     start(R_RY, y, at_y, lambda j: r_src.at[j], r_y.at[y])
     r_y[y] = r_src[y]
-    send(bas_hbm, bas_g.at[core, x], R_SIB + 0, sibling)
-    send(bas_g.at[core, x_down], bas_g.at[core, x_down], R_SIB + 1, sibling)
-    send(bas_g.at[core, x_up], bas_g.at[core, x_up], R_SIB + 2, sibling)
+    arrived(R_BAS + 0, bas_g.at[core, x_down, low])
+    basis(x_down, low, R_BAS + 4, x_up)
+    arrived(R_BAS + 1, bas_g.at[core, x_up, high])
+    basis(x_up, high, R_BAS + 5, x_down)
+    send(bas_g.at[core, x], bas_g.at[core, x], R_SIB + 0, sibling)
     finish(R_RY, y, lambda j: r_y.at[j])
     here = pl.ds(pl.multiple_of(16 * y, 16), 16)
     r_full[zh, :, here] = add4(r_y[0], r_y[1], r_y[2], r_y[3]).astype(BF16)
     start(R_RZ, zh, at_z, lambda j: r_full.at[zh, :, here], r_full.at[zh, :, here])
     start(R_RG + 4 * zh, y, at_y, lambda j: r_full.at[zh, :, here], r_full.at[zh, :, here])
-    arrived(R_BAS + 2, bas_g.at[core, x_far, 0:1024])
-    arrived(R_BAS + 3, bas_g.at[core, x_far, 1024:2048])
-    send(bas_g.at[core, x_far], bas_g.at[core, x_far], R_SIB + 3, sibling)
+    arrived(R_BAS + 2, bas_g.at[core, x_down, high])
+    send(bas_g.at[core, x_down], bas_g.at[core, x_down], R_SIB + 1, sibling)
+    arrived(R_BAS + 3, bas_g.at[core, x_up, low])
+    send(bas_g.at[core, x_up], bas_g.at[core, x_up], R_SIB + 2, sibling)
     for d in (1, 3, 2):
         z = (zh + d) % 4
         arrived(R_RZ + z, r_full.at[z, :, here])
         start(R_RG + 4 * z, y, at_y, lambda j: r_full.at[z, :, here], r_full.at[z, :, here])
+    arrived(R_BAS + 4, bas_g.at[core, x_far, low])
+    arrived(R_BAS + 5, bas_g.at[core, x_far, high])
+    send(bas_g.at[core, x_far], bas_g.at[core, x_far], R_SIB + 3, sibling)
     for d in (0, 1, 3, 2):
         z = (zh + d) % 4
         for e in (1, 3, 2):
@@ -344,7 +361,6 @@
         def _():
             turn(k).wait_send()
 
-    loads[3].wait()
     for j, slot in ((0, x), (1, x_down), (2, x_up), (3, x_far)):
         arrived(R_SIB + j, bas_g.at[1 - core, slot])
     own = []
@@ -392,41 +408,83 @@
     finish(R_QZ, zh, lambda j: q_z.at[j])
     piece = add4(q_z[0], q_z[1], q_z[2], q_z[3]).astype(BF16)
 
-    for half in range(2):
-        g_src[:, half] = piece[:, :, 256 * half:256 * (half + 1)]
-    ret[zh, :, x, core, y] = g_src[core]
+    def spot(z):
+        return pl.ds(pl.multiple_of(512 * z, 512), 512)
+
+    g_src[...] = piece
+    own_ret = pltpu.make_async_copy(g_src.at[core], ret.at[x, core, y, :, spot(zh)], lsem.at[8])
+    own_ret.start()
     for d in (2, 1, 3):
         j = (zh + d) % 4
         for k in (core, 1 - core):
-            send(g_src.at[k], ret.at[zh, :, x, core, y], R_GZ + 2 * zh + core, (at_z(j)[0], zlo * 2 + k))
-    send(g_src.at[1 - core], ret.at[zh, :, x, core, y], R_GZ + 2 * zh + core, sibling)
-    arrived(R_GZ + 2 * zh + 1 - core, ret.at[zh, :, x, 1 - core, y])
+            send(g_src.at[k], ret.at[x, core, y, :, spot(zh)], R_GZ + 2 * zh + core, (at_z(j)[0], zlo * 2 + k))
+    send(g_src.at[1 - core], ret.at[x, core, y, :, spot(zh)], R_GZ + 2 * zh + core, sibling)
+    arrived(R_GZ + 2 * zh + 1 - core, ret.at[x, 1 - core, y, :, spot(zh)])
     for d in (1, 3, 2):
         j = (zh + d) % 4
         for k in range(2):
-            arrived(R_GZ + 2 * j + k, ret.at[j, :, x, k, y])
-
-    start(R_GX, x, at_x, lambda j: ret.at[:, :, x, :, y], ret.at[:, :, x, :, y])
-    start(R_GY, y, at_y, lambda j: ret.at[:, :, x, :, y], ret.at[:, :, x, :, y])
-    for d in (1, 3, 2):
-        j = (y + d) % 4
-        arrived(R_GY + j, ret.at[:, :, x, :, j])
-        for e in (2, 1, 3):
-            send(ret.at[:, 0, x, :, j], ret.at[:, 0, x, :, j], R_FX + 4 * x + j, at_x((x + e) % 4))
-        j = (x + d) % 4
-        arrived(R_GX + j, ret.at[:, :, j, :, y])
-        for e in (2, 1, 3):
-            send(ret.at[:, 1, j, :, y], ret.at[:, 1, j, :, y], R_FY + 4 * j + y, at_y((y + e) % 4))
-    for half in range(2):
-        for d in (1, 3, 2):
-            for e in (1, 3, 2):
-                jx, jy = (x + e) % 4, (y + d) % 4
-                arrived((R_FX if half == 0 else R_FY) + 4 * jx + jy, ret.at[:, half, jx, :, jy])
-        for z in range(4):
-            acc = jnp.dot(h_win[0], ret[z, half, 0:2].reshape(256, 256), preferred_element_type=F32)
-            acc = acc + jnp.dot(h_win[1], ret[z, half, 2:4].reshape(256, 256), preferred_element_type=F32)
-            at = 512 * z + 256 * half
-            out_ref[:, at:at + 256] = acc.astype(BF16)
+            arrived(R_GZ + 2 * j + k, ret.at[x, k, y, :, spot(j)])
+    own_ret.wait()
+
+    whole, part_a, part_b = 0, 1, 2
+    y_up, y_down, y_far = (y + 1) % 4, (y + 3) % 4, (y + 2) % 4
+    x_ring = (x, x_up, x_down, x_far, at_x)
+    y_ring = (y, y_up, y_down, y_far, at_y)
+
+    def give_both(ring, base, block):
+        me, up, down, far, place = ring
+        send(block(me, whole), block(me, whole), base, place(up))
+        send(block(me, whole), block(me, whole), base + 1, place(down))
+
+    def pass_on(ring, base, block, side):
+        me, up, down, far, place = ring
+        if side == 0:
+            arrived(base, block(down, whole))
+            send(block(down, part_a), block(down, part_a), base + 2, place(up))
+        else:
+            arrived(base + 1, block(up, whole))
+            send(block(up, part_b), block(up, part_b), base + 3, place(down))
+
+    def take_far(ring, base, block):
+        me, up, down, far, place = ring
+        arrived(base + 2, block(far, part_a))
+        arrived(base + 3, block(far, part_b))
+
+    def gx(j, part):
+        return ret.at[j, :, y, :, (slice(0, 2048), slice(0, 1024), slice(1024, 2048))[part]]
+
+    def gy(j, part):
+        return ret.at[x, :, j, :, (slice(0, 2048), slice(0, 1024), slice(1024, 2048))[part]]
+
+    def fx(k):
+        return lambda j, part: ret.at[j, :, k, :, (slice(0, 1024), slice(0, 512), slice(512, 1024))[part]]
+
+    def fy(k):
+        return lambda j, part: ret.at[k, :, j, :, (slice(1024, 2048), slice(1024, 1536), slice(1536, 2048))[part]]
+
+    give_both(x_ring, R_GX, gx)
+    give_both(y_ring, R_GY, gy)
+    near = ((0, y_down, x_down), (1, y_up, x_up))
+    for side, ky, kx in near:
+        pass_on(y_ring, R_GY, gy, side)
+        give_both(x_ring, R_FX + 4 * side, fx(ky))
+        pass_on(x_ring, R_GX, gx, side)
+        give_both(y_ring, R_FY + 4 * side, fy(kx))
+    take_far(y_ring, R_GY, gy)
+    give_both(x_ring, R_FX + 8, fx(y_far))
+    take_far(x_ring, R_GX, gx)
+    give_both(y_ring, R_FY + 8, fy(x_far))
+    cols = ((0, y_down, x_down), (1, y_up, x_up), (2, y_far, x_far))
+    for n, ky, kx in cols:
+        for side in range(2):
+            pass_on(x_ring, R_FX + 4 * n, fx(ky), side)
+            pass_on(y_ring, R_FY + 4 * n, fy(kx), side)
+    for n, ky, kx in cols:
+        take_far(x_ring, R_FX + 4 * n, fx(ky))
+        take_far(y_ring, R_FY + 4 * n, fy(kx))
+    for cp in wins:
+        cp.wait()
+    assert used[0] <= N_SEND
     for cp in sends:
         cp.wait_send()
 
@@ -454,34 +512,35 @@
         name="pick",
     )(panel_order, hidden_basis, eigenvalues)
 
-    return pl.pallas_call(
+    ret, win = pl.pallas_call(
         kernel,
-        out_shape=jax.ShapeDtypeStruct((448, 2048), BF16),
-        in_specs=[hbm, hbm, hbm, hbm, hbm, vmem, vmem],
-        out_specs=vmem,
+        out_shape=[jax.ShapeDtypeStruct((4, 2, 4, 16, 2048), BF16), jax.ShapeDtypeStruct((448, 512), BF16)],
+        in_specs=[hbm] * 7,
+        out_specs=[hbm, hbm],
         scratch_shapes=[
             buf(448, 256), buf(256, 448), pltpu.VMEM((1, 256), jnp.int32), pltpu.VMEM((16, 128), F32),
             buf(2, 4, 256, 128), buf(2, 4, 2048, 128),
             buf(4, 128, 128), buf(4, 4, 64, 128),
-            buf(224, 256), buf(224, 256), buf(2, 448, 256),
+            buf(224, 256), buf(224, 256), buf(224, 256), buf(2, 448, 256),
             buf(2, 4, 64, 256), buf(2, 4, 64, 256), buf(4, 64, 128), buf(4, 64, 128), buf(64, 128), buf(4, 64, 128),
             buf(64, 128), buf(4, 64, 128),
             buf(2, 64, 256), buf(4, 2, 16, 512), buf(4, 2, 16, 512), buf(4, 2, 64, 512),
             buf(4, 64, 128), buf(4, 64, 128), buf(4, 64, 128),
-            buf(4, 4, 2, 16, 512), buf(4, 4, 2, 16, 512), buf(4, 2, 16, 512), buf(4, 2, 16, 512), buf(2, 2, 16, 256),
-            buf(4, 2, 4, 2, 4, 16, 256),
+            buf(4, 4, 2, 16, 512), buf(4, 4, 2, 16, 512), buf(4, 2, 16, 512), buf(4, 2, 16, 512), buf(2, 16, 512),
             pltpu.SemaphoreType.DMA((N_SEND,)),
             pltpu.SemaphoreType.DMA((N_RECV,)),
-            pltpu.SemaphoreType.DMA((6,)),
+            pltpu.SemaphoreType.DMA((11,)),
         ],
         compiler_params=pltpu.CompilerParams(
-            collective_id=0, has_side_effects=True, vmem_limit_bytes=60 * 1024 * 1024),
+            collective_id=0, has_side_effects=True, vmem_limit_bytes=50 * 1024 * 1024),
         cost_estimate=pl.CostEstimate(flops=3_000_000_000, bytes_accessed=12_000_000, transcendentals=0),
         name="influence",
     )(
         cotangent.T, activations, shard_of_token.reshape(1, 256), shard_weight.reshape(16, 128),
         input_basis, h_src, e_src,
     )
+
+    return jnp.dot(win, ret.reshape(512, 2048), preferred_element_type=F32).astype(BF16)
 
 
 def solution(mesh):

time: 103 us -> 95.8 us (0.930)
  the two profiles are of different devices: /device:TPU:1 before, /device:TPU:6 now
where the time goes in v3:
time: 95.8 us; the launch traced here: 95.7 us
  Pallas kernels  91.3 us (95%)
  matrix products  2.36 us (2%)
  local copies, waits for them, and re-layouts  1.94 us (2%)
    pallas_call x1, Pallas kernels, per_device(): pl.pallas_call(kernel, out_shape=[jax.ShapeDtypeStruct((4, 2, 4, 16, 2048...  89.6 us
    dot_general x1, matrix products, per_device(): jnp.dot(win, ret.reshape(512, 2048), preferred_element_type=F32)  2.36 us
    unnamed x14, local copies, waits for them, and re-layouts  1.94 us

profile of v3, /device:TPU:6, one launch (start us, length us, event | category | flops | bytes accessed | tf_op | source)
XLA Modules:
  0.0 95.7 jit_solution(7817104238502929253)
XLA Ops:
  0.0 0.0 copy-start
  0.0 0.0 copy-start.2
  0.0 0.0 copy-start.4
  0.0 0.0 copy-start.5
  0.0 0.0 copy-start.6
  0.0 1.7 %pick.1 = (bf16[2,448,256]{2,1,0:T(8,128)(2,1)}, bf16[512,128]{1,0:T(8,128)(2,1)}) custom-call(s32[2]{0:T(128)} %order_hbm.1, bf16[448,7168]{1,0:T(8,128)(2,1)} %hid_hbm.1, bf16[7168,128]{1,0:T(8,128)(2,1)} %eig_hbm.1), custom_call_target="tpu_custom_call" | custom-call | tf_op jit(solution)/shard_map/pick/pallas_call | solution.py:505
  1.7 0.0 copy-done
  1.7 0.0 copy-done.2
  1.8 0.0 copy-done.4
  1.8 0.0 copy-done.5
  1.8 0.0 copy-done.6
  1.8 0.0 copy-start.1
  1.8 1.0 %copy-done.1 = bf16[2,448,256]{2,1,0:T(8,128)(2,1)S(1)} copy-done((bf16[2,448,256]{2,1,0:T(8,128)(2,1)S(1)}, bf16[2,448,256]{2,1,0:T(8,128)(2,1)}, u32[]{:S(2)}) %copy-start.1) | copy-done | bytes 458776
  2.8 0.0 copy-start.3
  2.8 0.9 copy-done.3
  3.7 89.6 %influence.1 = (bf16[4,2,4,16,2048]{4,3,2,1,0:T(8,128)(2,1)S(1)}, bf16[448,512]{1,0:T(8,128)(2,1)S(1)}) custom-call(bf16[448,256]{1,0:T(8,128)(2,1)S(1)} %bitcast.6, bf16[256,128]{1,0:T(8,128)(2,1)S(1)} %copy-done.4, s32[1,256]{1,0:T(1,128)S(1)} %bitcast.8, f32[16,128]{1,0:T(8,128)S(1)} %bitcast.7, bf16[2048,128]{1,0:T(8,128)(2,1)S(1)} %copy-done, ...), custom_call_target="tpu_custom_call" | custom-call | flops 3000000000 | bytes 12000000 | tf_op jit(solution)/shard_map/influence/pallas_call | solution.py:515
  93.3 2.4 %convolution_convert_fusion = bf16[448,2048]{1,0:T(8,128)(2,1)} fusion(bf16[448,512]{1,0:T(8,128)(2,1)S(1)} %get-tuple-element.11, bf16[512,2048]{1,0:T(8,128)(2,1)S(1)} %bitcast.9), kind=kOutput, calls=%fused_computation | convolution fusion | flops 940441600 | bytes 4390912 | tf_op jit(solution)/shard_map/dot_general | solution.py:543
Async XLA Ops:
  0.0 1.7 %copy-start = (bf16[2048,128]{1,0:T(8,128)(2,1)S(1)}, bf16[2048,128]{1,0:T(8,128)(2,1)}, u32[]{:S(2)}) copy-start(bf16[2048,128]{1,0:T(8,128)(2,1)} %bas_hbm.1) | copy-start | bytes 1572868
  0.0 1.7 %copy-start.2 = (bf16[256,448]{0,1:T(8,128)(2,1)S(1)}, bf16[256,448]{0,1:T(8,128)(2,1)}, u32[]{:S(2)}) copy-start(bf16[256,448]{0,1:T(8,128)(2,1)} %param.8) | copy-start | bytes 688132
  0.0 1.8 %copy-start.4 = (bf16[256,128]{1,0:T(8,128)(2,1)S(1)}, bf16[256,128]{1,0:T(8,128)(2,1)}, u32[]{:S(2)}) copy-start(bf16[256,128]{1,0:T(8,128)(2,1)} %act_hbm.1) | copy-start | bytes 196612
  0.0 1.8 %copy-start.5 = (f32[2048]{0:T(1024)S(1)}, f32[2048]{0:T(1024)}, u32[]{:S(2)}) copy-start(f32[2048]{0:T(1024)} %param.11) | copy-start | bytes 24580
  0.0 1.8 %copy-start.6 = (s32[256]{0:T(256)S(1)}, s32[256]{0:T(256)}, u32[]{:S(2)}) copy-start(s32[256]{0:T(256)} %param.10) | copy-start | bytes 3076
  1.8 1.0 %copy-start.1 = (bf16[2,448,256]{2,1,0:T(8,128)(2,1)S(1)}, bf16[2,448,256]{2,1,0:T(8,128)(2,1)}, u32[]{:S(2)}) copy-start(bf16[2,448,256]{2,1,0:T(8,128)(2,1)} %get-tuple-element.9.h_src) | copy-start | bytes 1376260
  2.8 0.9 copy-start.3

commit v4 on v3

--- a/solution.py
+++ b/solution.py
@@ -508,9 +508,9 @@
         in_specs=[hbm, hbm, hbm],
         out_specs=[vmem, vmem],
         scratch_shapes=[pltpu.SMEM((2,), jnp.int32), pltpu.SemaphoreType.DMA((5,))],
-        compiler_params=pltpu.CompilerParams(vmem_limit_bytes=60 * 1024 * 1024),
+        compiler_params=pltpu.CompilerParams(vmem_limit_bytes=40 * 1024 * 1024),
         name="pick",
-    )(panel_order, hidden_basis, eigenvalues)
+    )(*[pltpu.with_memory_space_constraint(a, pltpu.HBM) for a in (panel_order, hidden_basis, eigenvalues)])
 
     ret, win = pl.pallas_call(
         kernel,
@@ -535,10 +535,10 @@
             collective_id=0, has_side_effects=True, vmem_limit_bytes=50 * 1024 * 1024),
         cost_estimate=pl.CostEstimate(flops=3_000_000_000, bytes_accessed=12_000_000, transcendentals=0),
         name="influence",
-    )(
-        cotangent.T, activations, shard_of_token.reshape(1, 256), shard_weight.reshape(16, 128),
-        input_basis, h_src, e_src,
-    )
+    )(*[
+        pltpu.with_memory_space_constraint(a, pltpu.HBM)
+        for a in (cotangent.T, activations, shard_of_token.reshape(1, 256), shard_weight.reshape(16, 128), input_basis)
+    ] + [h_src, e_src])
 
     return jnp.dot(win, ret.reshape(512, 2048), preferred_element_type=F32).astype(BF16)
 

time: 95.8 us -> 93.1 us (0.972)
  local copies, waits for them, and re-layouts: 1.94 us -> 0 us
    unnamed x14 -> x0, local copies, waits for them, and re-layouts: 1.94 us -> none
where the time goes in v4:
time: 93.1 us; the launch traced here: 93 us
  Pallas kernels  90.6 us (97%)
  matrix products  2.36 us (3%)
    pallas_call x1, Pallas kernels, per_device(): pl.pallas_call(kernel, out_shape=[jax.ShapeDtypeStruct((4, 2, 4, 16, 2048...  89.9 us
    dot_general x1, matrix products, per_device(): jnp.dot(win, ret.reshape(512, 2048), preferred_element_type=F32)  2.36 us

profile of v4, /device:TPU:6, one launch (start us, length us, event | category | flops | bytes accessed | tf_op | source)
XLA Modules:
  0.0 93.0 jit_solution(1756158573134489374)
XLA Ops:
  0.0 0.8 pick.1
  0.8 89.9 %influence.1 = (bf16[4,2,4,16,2048]{4,3,2,1,0:T(8,128)(2,1)S(1)}, bf16[448,512]{1,0:T(8,128)(2,1)S(1)}) custom-call(bf16[448,256]{1,0:T(8,128)(2,1)} %bitcast.7, bf16[256,128]{1,0:T(8,128)(2,1)} %act_hbm.1, s32[1,256]{1,0:T(1,128)} %bitcast.9, f32[16,128]{1,0:T(8,128)} %bitcast.8, bf16[2048,128]{1,0:T(8,128)(2,1)} %bas_hbm.1, ...), custom_call_target="tpu_custom_call" | custom-call | flops 3000000000 | bytes 12000000 | tf_op jit(solution)/shard_map/influence/pallas_call | solution.py:515
  90.6 2.4 %convolution_convert_fusion = bf16[448,2048]{1,0:T(8,128)(2,1)} fusion(bf16[448,512]{1,0:T(8,128)(2,1)S(1)} %get-tuple-element.11, bf16[512,2048]{1,0:T(8,128)(2,1)S(1)} %bitcast.6), kind=kOutput, calls=%fused_computation | convolution fusion | flops 940441600 | bytes 4390912 | tf_op jit(solution)/shard_map/dot_general | solution.py:543

commit v5 on v4

--- a/solution.py
+++ b/solution.py
@@ -272,6 +272,7 @@
     loads[3].wait()
     basis(x, low, R_BAS + 0, x_up)
     basis(x, high, R_BAS + 1, x_down)
+    send(bas_g.at[core, x], bas_g.at[core, x], R_SIB + 0, sibling)
     p_z0[...] = add4(p_x[0], p_x[1], p_x[2], p_x[3]).astype(BF16)
     start(R_PZ, zh, at_z, lambda j: p_z0, p_z.at[zh])
     p_z[zh] = p_z0[...]
@@ -304,6 +305,10 @@
         def _():
             p_g[y] = p_s[...]
 
+    arrived(R_BAS + 0, bas_g.at[core, x_down, low])
+    basis(x_down, low, R_BAS + 4, x_up)
+    arrived(R_BAS + 1, bas_g.at[core, x_up, high])
+    basis(x_up, high, R_BAS + 5, x_down)
     loads[5].wait()
     finish(R_EIX, x, lambda j: e_x.at[j])
     for d in (2, 1, 3):
@@ -329,11 +334,6 @@
                 r_src[k, q, :, 128 * j:128 * (j + 1)] = part[16 * k:16 * (k + 1)]
     start(R_RY, y, at_y, lambda j: r_src.at[j], r_y.at[y])
     r_y[y] = r_src[y]
-    arrived(R_BAS + 0, bas_g.at[core, x_down, low])
-    basis(x_down, low, R_BAS + 4, x_up)
-    arrived(R_BAS + 1, bas_g.at[core, x_up, high])
-    basis(x_up, high, R_BAS + 5, x_down)
-    send(bas_g.at[core, x], bas_g.at[core, x], R_SIB + 0, sibling)
     finish(R_RY, y, lambda j: r_y.at[j])
     here = pl.ds(pl.multiple_of(16 * y, 16), 16)
     r_full[zh, :, here] = add4(r_y[0], r_y[1], r_y[2], r_y[3]).astype(BF16)

time: 93.1 us -> 93.1 us (level); the launches traced: 93 us -> 91.9 us
  Pallas kernels: 90.6 us -> 89.5 us
    pallas_call x1, Pallas kernels: 89.9 us -> 88.8 us  [per_device(): pl.pallas_call(kernel, out_shape=[jax.ShapeDtypeStruct((4, 2, 4, 16, 2048...]
where the time goes in v5:
time: 93.1 us; the launch traced here: 91.9 us
  Pallas kernels  89.5 us (96%)
  matrix products  2.36 us (3%)
    pallas_call x1, Pallas kernels, per_device(): pl.pallas_call(kernel, out_shape=[jax.ShapeDtypeStruct((4, 2, 4, 16, 2048...  88.8 us
    dot_general x1, matrix products, per_device(): jnp.dot(win, ret.reshape(512, 2048), preferred_element_type=F32)  2.36 us

profile of v5, /device:TPU:6, one launch (start us, length us, event | category | flops | bytes accessed | tf_op | source)
XLA Modules:
  0.0 91.9 jit_solution(16327923086033583115)
XLA Ops:
  0.0 0.8 pick.1
  0.8 88.8 %influence.1 = (bf16[4,2,4,16,2048]{4,3,2,1,0:T(8,128)(2,1)S(1)}, bf16[448,512]{1,0:T(8,128)(2,1)S(1)}) custom-call(bf16[448,256]{1,0:T(8,128)(2,1)} %bitcast.7, bf16[256,128]{1,0:T(8,128)(2,1)} %act_hbm.1, s32[1,256]{1,0:T(1,128)} %bitcast.9, f32[16,128]{1,0:T(8,128)} %bitcast.8, bf16[2048,128]{1,0:T(8,128)(2,1)} %bas_hbm.1, ...), custom_call_target="tpu_custom_call" | custom-call | flops 3000000000 | bytes 12000000 | tf_op jit(solution)/shard_map/influence/pallas_call | solution.py:515
  89.5 2.4 %convolution_convert_fusion = bf16[448,2048]{1,0:T(8,128)(2,1)} fusion(bf16[448,512]{1,0:T(8,128)(2,1)S(1)} %get-tuple-element.11, bf16[512,2048]{1,0:T(8,128)(2,1)S(1)} %bitcast.6), kind=kOutput, calls=%fused_computation | convolution fusion | flops 940441600 | bytes 4390912 | tf_op jit(solution)/shard_map/dot_general | solution.py:543
